TPU v7x, 32 devices: a whole 2x2x4 slice. The times are simulated.
32 devices in a mesh: band: 2 (over y), lon: 16 (over z, x, core).
Axes of the slice: x: 2, y: 2, z: 4, core: 2. Of those that a mesh axis runs over, the one named last changes fastest.
Arguments:
- tracers: float32 [96, 256, 128], P('band', 'lon'), may hold values from -6 to 6
- lon_offset: int32 [96, 4], P('band'), may hold values from -128 to 127
- lon_weights: float32 [4, 96, 4], P(None, 'band'), may hold values from -0.1 to 1, as said below
- lat_offset: int32 [96, 4], P('band'), may hold values from -6 to 6
- lat_weights: float32 [4, 96, 4], P(None, 'band'), may hold values from -0.1 to 1, as said below
Outputs:
- advected: float32 [96, 256, 128], P('band', 'lon')
Inputs may be any that keep to these rules, and one draw needn't show every extreme that they name: `lon_weights`: each set of four weights sums to one. `lat_weights`: each set of four weights sums to one.
All inputs are finite; a program needn't handle non-finite values.
Results may differ from a plain program's by a relative error of at most 0.0003.
Values sent between devices are 32-bit elements; how exact they have to be, the bound alone decides.
A program may use at most 64 MiB of HBM per device.

v0:
```python
import jax
import jax.numpy as jnp
from jax import lax
from jax.sharding import PartitionSpec as P

TMAX = 6


def passed_along(value, axis, steps):
    count = lax.axis_size(axis)
    pairs = [(source, (source + steps) % count) for source in range(count)]
    return lax.ppermute(value, axis, pairs)


def extended_2(cells, sides, width, closed):
    for axis, dim in sides:
        count = lax.axis_size(axis)
        ends = count if closed else count - 1
        head = lax.slice_in_dim(cells, 0, width, axis=dim)
        tail = lax.slice_in_dim(cells, cells.shape[dim] - width, cells.shape[dim], axis=dim)
        cells = jnp.concatenate(
            [
                lax.ppermute(tail, axis, [(i, (i + 1) % count) for i in range(ends)]),
                cells,
                lax.ppermute(head, axis, [((i + 1) % count, i) for i in range(ends)]),
            ],
            axis=dim,
        )
    return cells


def spread_levels(values, per_level):
    return jnp.repeat(values, per_level, axis=-1)


def zonal_pass(field, offsets, weights):
    rows, width, columns = field.shape
    levels = offsets.shape[1]
    per_level = columns // levels
    sectors = lax.axis_size("lon")
    circle = width * sectors
    wrapped = jnp.mod(offsets, circle)
    steps = spread_levels(wrapped // width, per_level)
    rest = spread_levels(wrapped % width, per_level)
    coeffs = spread_levels(weights, per_level)
    moved = field
    for bit in range(sectors.bit_length() - 1):
        other = passed_along(moved, "lon", 1 << bit)
        taken = steps // (1 << bit) % 2 == 1
        moved = jnp.where(taken[:, None, :], other, moved)
    extended = extended_2(moved, (("lon", 1),), width, True)
    target = jnp.arange(width, dtype=jnp.int32)[None, :, None, None]
    source = jnp.arange(3 * width, dtype=jnp.int32)[None, None, :, None]
    base = (width - 1 - rest)[:, None, None, :]
    banded = jnp.zeros((rows, width, 3 * width, columns), jnp.float32)
    for k in range(4):
        banded = banded + coeffs[k][:, None, None, :] * (source == target + base + k).astype(
            jnp.float32
        )
    return jnp.sum(banded * extended[:, None, :, :], axis=2)


def meridional_pass(field, offsets, weights, form, per_level):
    rows = field.shape[0]
    reach = TMAX + 2
    extended = extended_2(field, (("band", 0),), reach, False)
    total_rows = rows * lax.axis_size("band")
    first_row = lax.axis_index("band") * rows
    glob = first_row + jnp.arange(rows, dtype=jnp.int32)[:, None]
    places = jnp.arange(rows + 2 * reach, dtype=jnp.int32)[None, :, None]
    selector = jnp.zeros((rows, rows + 2 * reach, offsets.shape[1]), jnp.float32)
    for k in range(4):
        source = jnp.clip(glob - offsets + (k - 1), 0, total_rows - 1) - first_row + reach
        selector = selector + weights[k][:, None, :] * (places == source[:, None, :]).astype(
            jnp.float32
        )
    selector = spread_levels(selector, per_level)
    return jnp.einsum(form, selector, extended, precision=lax.Precision.HIGHEST)


def per_device(tracers, lon_offset, lon_weights, lat_offset, lat_weights):
    rows, width, columns = tracers.shape
    levels = lon_offset.shape[1]
    first = zonal_pass(tracers, lon_offset, lon_weights)
    second = meridional_pass(first, lat_offset, lat_weights, "jpc,pic->jic", columns // levels)
    return zonal_pass(second, lon_offset, lon_weights)


def solution(mesh):
    return jax.shard_map(
        per_device,
        mesh=mesh,
        in_specs=(
            P("band", "lon", None),
            P("band", None),
            P(None, "band", None),
            P("band", None),
            P(None, "band", None),
        ),
        out_specs=P("band", "lon", None),
        check_vma=False,
    )
```

profile of v0, /device:TPU:0, one launch (start us, length us, event | category | flops | bytes accessed | tf_op | source)
XLA Modules:
  0.0 175.7 jit_solution(6719290671832153994)
XLA Ops:
  0.0 0.5 collective-permute-start
  0.5 1.5 copy.61
  2.0 0.7 fusion.37
  2.8 8.3 %collective-permute-done = f32[48,16,128]{2,1,0:T(8,128)S(1)} collective-permute-done((f32[48,16,128]{2,1,0:T(8,128)}, f32[48,16,128]{2,1,0:T(8,128)S(1)}, u32[]{:S(2)}, u32[]{:S(2)}) %collective-permute-start) | collective-permute-done | bytes 393248 | tf_op jit(solution)/shard_map/ppermute | solution.py:12
  11.1 0.6 copy.60
  11.7 0.2 broadcast_select_fusion.1
  11.8 0.5 copy.62
  12.4 10.7 %collective-permute-done.1 = f32[48,16,128]{2,1,0:T(8,128)S(1)} collective-permute-done((f32[48,16,128]{2,1,0:T(8,128)S(1)}, f32[48,16,128]{2,1,0:T(8,128)S(1)}, u32[]{:S(2)}, u32[]{:S(2)}) %collective-permute-start.1) | collective-permute-done | bytes 393248 | tf_op jit(solution)/shard_map/ppermute | solution.py:12
  23.1 0.6 copy.63
  23.7 0.2 broadcast_select_fusion.3
  23.9 0.5 copy.64
  24.5 10.2 %collective-permute-done.2 = f32[48,16,128]{2,1,0:T(8,128)S(1)} collective-permute-done((f32[48,16,128]{2,1,0:T(8,128)S(1)}, f32[48,16,128]{2,1,0:T(8,128)S(1)}, u32[]{:S(2)}, u32[]{:S(2)}) %collective-permute-start.2) | collective-permute-done | bytes 393248 | tf_op jit(solution)/shard_map/ppermute | solution.py:12
  34.7 0.6 copy.65
  35.3 0.2 broadcast_select_fusion.5
  35.5 0.5 copy.66
  36.0 0.1 collective-permute-start.3
  36.1 0.7 copy.56
  36.8 0.7 copy.55
  37.5 0.7 copy.57
  38.2 0.7 copy.59
  38.9 0.7 copy.58
  39.6 0.6 subtract_add_fusion.3
  40.2 10.7 %collective-permute-done.3 = f32[48,16,128]{2,1,0:T(8,128)S(1)} collective-permute-done((f32[48,16,128]{2,1,0:T(8,128)S(1)}, f32[48,16,128]{2,1,0:T(8,128)S(1)}, u32[]{:S(2)}, u32[]{:S(2)}) %collective-permute-start.3) | collective-permute-done | bytes 393248 | tf_op jit(solution)/shard_map/ppermute | solution.py:12
  50.9 0.6 copy.67
  51.5 0.2 broadcast_select_fusion.7
  51.7 0.5 copy.68
  52.2 1.1 collective-permute-start.5
  53.3 0.8 iota_add_fusion
  54.2 4.4 %collective-permute-done.5 = f32[48,16,128]{2,1,0:T(8,128)S(1)} collective-permute-done((f32[48,16,128]{2,1,0:T(8,128)S(1)}, f32[48,16,128]{2,1,0:T(8,128)S(1)}, u32[]{:S(2)}, u32[]{:S(2)}) %collective-permute-start.5) | collective-permute-done | bytes 393248 | tf_op jit(solution)/shard_map/ppermute | solution.py:25
  58.6 4.7 %collective-permute-done.4 = f32[48,16,128]{2,1,0:T(8,128)S(1)} collective-permute-done((f32[48,16,128]{2,1,0:T(8,128)S(1)}, f32[48,16,128]{2,1,0:T(8,128)S(1)}, u32[]{:S(2)}, u32[]{:S(2)}) %collective-permute-start.4) | collective-permute-done | bytes 393248 | tf_op jit(solution)/shard_map/ppermute | solution.py:23
  63.3 0.1 pad_maximum_fusion
  63.4 14.1 %multiply_reduce_fusion.1 = f32[48,16,128]{2,1,0:T(8,128)S(1)} fusion(f32[48,48,128]{2,1,0:T(8,128)S(1)} %pad_maximum_fusion, f32[48,128]{1,0:T(8,128)S(1)} %copy-done.9, s32[48,16,128]{2,1,0:T(8,128)S(1)} %get-tuple-element.8, f32[48,128]{1,0:T(8,128)S(1)} %copy-done.10, s32[48,16,128]{2,1,0:T(8,128)S(1)} %get-tuple-element.9, f32[48,128]{1,0:T(8,128)S(1)} %copy-done.8, ...), kind=kLoop, calls=%fused_computation.1 | loop fusion | flops 61243392 | bytes 3244032 | tf_op jit(solution)/shard_map/reduce_sum | solution.py:60
  77.5 3.4 %collective-permute-start.6 = (f32[8,16,128]{2,1,0:T(8,128)S(1)}, f32[8,16,128]{2,1,0:T(8,128)S(1)}, u32[]{:S(2)}, u32[]{:S(2)}) collective-permute-start(f32[8,16,128]{2,1,0:T(8,128)S(1)} %get-tuple-element.5), channel_id=1, source_target_pairs={{0,16},{1,17},{2,18},{3,19},{4,20},{5,21},{6,22},{7,23},{8,24},{9,... | collective-permute-start | bytes 196616 | tf_op jit(solution)/shard_map/ppermute | solution.py:23
  80.9 1.5 collective-permute-start.7
  82.5 0.3 select_add_fusion.1
  82.7 0.6 copy.72
  83.3 3.9 %collective-permute-done.7 = f32[8,16,128]{2,1,0:T(8,128)S(1)} collective-permute-done((f32[8,16,128]{2,1,0:T(8,128)S(1)}, f32[8,16,128]{2,1,0:T(8,128)S(1)}, u32[]{:S(2)}, u32[]{:S(2)}) %collective-permute-start.7) | collective-permute-done | bytes 65568 | tf_op jit(solution)/shard_map/ppermute | solution.py:25
  87.2 0.5 copy.73
  87.7 1.4 copy.71
  89.1 0.2 broadcast_in_dim.100
  89.3 1.0 copy-done
  90.3 5.1 %convolution_bitcast_fusion = f32[48,16,128]{0,1,2:T(8,128)S(1)} fusion(f32[48,64,128]{1,0,2:T(8,128)S(1)} %bitcast.118, f32[8,16,128]{0,1,2:T(8,128)S(1)} %copy.73, f32[48,16,128]{0,1,2:T(8,128)S(1)} %copy.72, f32[8,16,128]{0,1,2:T(8,128)S(1)} %copy-done), kind=kOutput, calls=%fused_computation.7 | convolution fusion | flops 75759616 | bytes 2490368 | tf_op jit(solution)/shard_map/jpc,pic->jic/dot_general | solution.py:78
  95.4 0.5 copy.74
  96.0 9.9 %collective-permute-done.8 = f32[48,16,128]{2,1,0:T(8,128)S(1)} collective-permute-done((f32[48,16,128]{2,1,0:T(8,128)S(1)}, f32[48,16,128]{2,1,0:T(8,128)S(1)}, u32[]{:S(2)}, u32[]{:S(2)}) %collective-permute-start.8) | collective-permute-done | bytes 393248 | tf_op jit(solution)/shard_map/ppermute | solution.py:12
  105.9 0.6 copy.75
  106.4 0.9 broadcast_select_fusion
  107.3 0.5 copy.76
  107.9 10.5 %collective-permute-done.9 = f32[48,16,128]{2,1,0:T(8,128)S(1)} collective-permute-done((f32[48,16,128]{2,1,0:T(8,128)S(1)}, f32[48,16,128]{2,1,0:T(8,128)S(1)}, u32[]{:S(2)}, u32[]{:S(2)}) %collective-permute-start.9) | collective-permute-done | bytes 393248 | tf_op jit(solution)/shard_map/ppermute | solution.py:12
  118.4 0.6 copy.77
  118.9 0.9 broadcast_select_fusion.2
  119.8 0.5 copy.78
  120.4 9.6 %collective-permute-done.10 = f32[48,16,128]{2,1,0:T(8,128)S(1)} collective-permute-done((f32[48,16,128]{2,1,0:T(8,128)S(1)}, f32[48,16,128]{2,1,0:T(8,128)S(1)}, u32[]{:S(2)}, u32[]{:S(2)}) %collective-permute-start.10) | collective-permute-done | bytes 393248 | tf_op jit(solution)/shard_map/ppermute | solution.py:12
  130.0 0.6 copy.79
  130.5 0.9 broadcast_select_fusion.4
  131.4 0.5 copy.80
  132.0 16.1 %collective-permute-done.11 = f32[48,16,128]{2,1,0:T(8,128)S(1)} collective-permute-done((f32[48,16,128]{2,1,0:T(8,128)S(1)}, f32[48,16,128]{2,1,0:T(8,128)S(1)}, u32[]{:S(2)}, u32[]{:S(2)}) %collective-permute-start.11) | collective-permute-done | bytes 393248 | tf_op jit(solution)/shard_map/ppermute | solution.py:12
  148.1 0.6 copy.81
  148.7 0.2 broadcast_select_fusion.6
  148.9 0.5 copy.82
  149.5 0.5 collective-permute-start.12
  150.0 4.8 %collective-permute-done.13 = f32[48,16,128]{2,1,0:T(8,128)S(1)} collective-permute-done((f32[48,16,128]{2,1,0:T(8,128)S(1)}, f32[48,16,128]{2,1,0:T(8,128)S(1)}, u32[]{:S(2)}, u32[]{:S(2)}) %collective-permute-start.13) | collective-permute-done | bytes 393248 | tf_op jit(solution)/shard_map/ppermute | solution.py:25
  154.8 5.0 %collective-permute-done.12 = f32[48,16,128]{2,1,0:T(8,128)S(1)} collective-permute-done((f32[48,16,128]{2,1,0:T(8,128)S(1)}, f32[48,16,128]{2,1,0:T(8,128)S(1)}, u32[]{:S(2)}, u32[]{:S(2)}) %collective-permute-start.12) | collective-permute-done | bytes 393248 | tf_op jit(solution)/shard_map/ppermute | solution.py:23
  159.8 0.1 pad_maximum_fusion.1
  159.9 15.8 %multiply_reduce_fusion = f32[48,16,128]{2,1,0:T(8,128)} fusion(f32[48,48,128]{2,1,0:T(8,128)S(1)} %pad_maximum_fusion.1, f32[48,128]{1,0:T(8,128)} %copy.59, s32[48,16,128]{2,1,0:T(8,128)S(1)} %copy-done.2, f32[48,128]{1,0:T(8,128)} %copy.58, s32[48,16,128]{2,1,0:T(8,128)S(1)} %copy-done.4, f32[48,128]{1,0:T(8,128)} %copy.57, s32[48,16,128]{2,1,0:T(8,128)S(1)} %copy-done.6, ...), kind=kLoop, calls=%fused_computation | loop fusion | flops 61243392 | bytes 3244032 | tf_op jit(solution)/shard_map/reduce_sum | solution.py:60
  (60 shorter events, 0.6 us)
Async XLA Ops:
  0.0 11.1 %collective-permute-start = (f32[48,16,128]{2,1,0:T(8,128)}, f32[48,16,128]{2,1,0:T(8,128)S(1)}, u32[]{:S(2)}, u32[]{:S(2)}) collective-permute-start(f32[48,16,128]{2,1,0:T(8,128)} %param.5), channel_id=1, source_target_pairs={{0,1},{1,2},{2,3},{3,4},{4,5},{5,6},{6,7},{7,8},{8,9},{9,10},{10,1... | collective-permute-start | bytes 1179656 | tf_op jit(solution)/shard_map/ppermute | solution.py:12
  2.8 20.9 %copy-start.13 = (pred[48,128]{0,1:T(8,128)(4,1)}, pred[48,128]{0,1:T(8,128)(4,1)S(1)}, u32[]{:S(2)}) copy-start(pred[48,128]{0,1:T(8,128)(4,1)S(1)} %get-tuple-element.28) | copy-start | bytes 18436
  2.8 20.9 %copy-start.12 = (pred[48,128]{0,1:T(8,128)(4,1)}, pred[48,128]{0,1:T(8,128)(4,1)S(1)}, u32[]{:S(2)}) copy-start(pred[48,128]{0,1:T(8,128)(4,1)S(1)} %get-tuple-element.27) | copy-start | bytes 18436
  2.8 32.5 %copy-start.11 = (pred[48,128]{0,1:T(8,128)(4,1)}, pred[48,128]{0,1:T(8,128)(4,1)S(1)}, u32[]{:S(2)}) copy-start(pred[48,128]{0,1:T(8,128)(4,1)S(1)} %get-tuple-element.26) | copy-start | bytes 18436
  12.3 10.8 %collective-permute-start.1 = (f32[48,16,128]{2,1,0:T(8,128)S(1)}, f32[48,16,128]{2,1,0:T(8,128)S(1)}, u32[]{:S(2)}, u32[]{:S(2)}) collective-permute-start(f32[48,16,128]{2,1,0:T(8,128)S(1)} %copy.62), channel_id=1, source_target_pairs={{0,2},{1,3},{2,4},{3,5},{4,6},{5,7},{6,8},{7,9},{8,10},{9,11},{10,... | collective-permute-start | bytes 1179656 | tf_op jit(solution)/shard_map/ppermute | solution.py:12
  24.4 11.7 %copy-start.18 = (f32[4,48,4]{1,2,0:T(4,128)S(1)}, f32[4,48,4]{1,2,0:T(4,128)}, u32[]{:S(2)}) copy-start(f32[4,48,4]{1,2,0:T(4,128)} %param.7) | copy-start | bytes 9220
  24.4 15.2 %copy-start.20 = (s32[48,4]{0,1:T(4,128)S(1)}, s32[48,4]{0,1:T(4,128)}, u32[]{:S(2)}) copy-start(s32[48,4]{0,1:T(4,128)} %param.8) | copy-start | bytes 2308
  24.4 10.3 %collective-permute-start.2 = (f32[48,16,128]{2,1,0:T(8,128)S(1)}, f32[48,16,128]{2,1,0:T(8,128)S(1)}, u32[]{:S(2)}, u32[]{:S(2)}) collective-permute-start(f32[48,16,128]{2,1,0:T(8,128)S(1)} %copy.64), channel_id=1, source_target_pairs={{0,4},{1,5},{2,6},{3,7},{4,8},{5,9},{6,10},{7,11},{8,12},{9,13},{1... | collective-permute-start | bytes 1179656 | tf_op jit(solution)/shard_map/ppermute | solution.py:12
  36.0 14.9 %collective-permute-start.3 = (f32[48,16,128]{2,1,0:T(8,128)S(1)}, f32[48,16,128]{2,1,0:T(8,128)S(1)}, u32[]{:S(2)}, u32[]{:S(2)}) collective-permute-start(f32[48,16,128]{2,1,0:T(8,128)S(1)} %copy.66), channel_id=1, source_target_pairs={{0,8},{1,9},{2,10},{3,11},{4,12},{5,13},{6,14},{7,15},{8,0},{9,1},... | collective-permute-start | bytes 1179656 | tf_op jit(solution)/shard_map/ppermute | solution.py:12
  38.2 15.1 %copy-start.19 = (f32[4,48,4]{1,2,0:T(4,128)S(1)}, f32[4,48,4]{1,2,0:T(4,128)}, u32[]{:S(2)}) copy-start(f32[4,48,4]{1,2,0:T(4,128)} %param.9) | copy-start | bytes 9220
  51.7 11.7 %copy-start.7 = (f32[48,128]{1,0:T(8,128)S(1)}, f32[48,128]{1,0:T(8,128)}, u32[]{:S(2)}) copy-start(f32[48,128]{1,0:T(8,128)} %copy.56) | copy-start | bytes 73732
  51.7 11.7 %copy-start.8 = (f32[48,128]{1,0:T(8,128)S(1)}, f32[48,128]{1,0:T(8,128)}, u32[]{:S(2)}) copy-start(f32[48,128]{1,0:T(8,128)} %copy.57) | copy-start | bytes 73732
  51.7 11.7 %copy-start.9 = (f32[48,128]{1,0:T(8,128)S(1)}, f32[48,128]{1,0:T(8,128)}, u32[]{:S(2)}) copy-start(f32[48,128]{1,0:T(8,128)} %copy.59) | copy-start | bytes 73732
  51.7 11.7 %copy-start.10 = (f32[48,128]{1,0:T(8,128)S(1)}, f32[48,128]{1,0:T(8,128)}, u32[]{:S(2)}) copy-start(f32[48,128]{1,0:T(8,128)} %copy.58) | copy-start | bytes 73732
  52.2 6.4 %collective-permute-start.5 = (f32[48,16,128]{2,1,0:T(8,128)S(1)}, f32[48,16,128]{2,1,0:T(8,128)S(1)}, u32[]{:S(2)}, u32[]{:S(2)}) collective-permute-start(f32[48,16,128]{2,1,0:T(8,128)S(1)} %copy.68), channel_id=1, source_target_pairs={{1,0},{2,1},{3,2},{4,3},{5,4},{6,5},{7,6},{8,7},{9,8},{10,9},{11,1... | collective-permute-start | bytes 1179656 | tf_op jit(solution)/shard_map/ppermute | solution.py:25
  53.3 10.0 %collective-permute-start.4 = (f32[48,16,128]{2,1,0:T(8,128)S(1)}, f32[48,16,128]{2,1,0:T(8,128)S(1)}, u32[]{:S(2)}, u32[]{:S(2)}) collective-permute-start(f32[48,16,128]{2,1,0:T(8,128)S(1)} %copy.68), channel_id=1, source_target_pairs={{0,1},{1,2},{2,3},{3,4},{4,5},{5,6},{6,7},{7,8},{8,9},{9,10},{10,1... | collective-permute-start | bytes 1179656 | tf_op jit(solution)/shard_map/ppermute | solution.py:23
  54.1 28.3 %copy-start.1 = (s32[48,16,128]{2,1,0:T(8,128)}, s32[48,16,128]{2,1,0:T(8,128)S(1)}, u32[]{:S(2)}) copy-start(s32[48,16,128]{2,1,0:T(8,128)S(1)} %get-tuple-element.8) | copy-start | bytes 1179652
  54.2 28.3 %copy-start.3 = (s32[48,16,128]{2,1,0:T(8,128)}, s32[48,16,128]{2,1,0:T(8,128)S(1)}, u32[]{:S(2)}) copy-start(s32[48,16,128]{2,1,0:T(8,128)S(1)} %get-tuple-element.9) | copy-start | bytes 1179652
  54.2 28.3 %copy-start.5 = (s32[48,16,128]{2,1,0:T(8,128)}, s32[48,16,128]{2,1,0:T(8,128)S(1)}, u32[]{:S(2)}) copy-start(s32[48,16,128]{2,1,0:T(8,128)S(1)} %get-tuple-element.10) | copy-start | bytes 1179652
  54.2 28.3 %copy-start.14 = (s32[48,4]{0,1:T(4,128)S(1)}, s32[48,4]{0,1:T(4,128)}, u32[]{:S(2)}) copy-start(s32[48,4]{0,1:T(4,128)} %get-tuple-element.19) | copy-start | bytes 2308
  54.2 28.3 %copy-start.15 = (s32[48,4]{0,1:T(4,128)S(1)}, s32[48,4]{0,1:T(4,128)}, u32[]{:S(2)}) copy-start(s32[48,4]{0,1:T(4,128)} %get-tuple-element.20) | copy-start | bytes 2308
  54.2 28.3 %copy-start.16 = (s32[48,4]{0,1:T(4,128)S(1)}, s32[48,4]{0,1:T(4,128)}, u32[]{:S(2)}) copy-start(s32[48,4]{0,1:T(4,128)} %get-tuple-element.21) | copy-start | bytes 2308
  54.2 28.3 %copy-start.17 = (s32[48,4]{0,1:T(4,128)S(1)}, s32[48,4]{0,1:T(4,128)}, u32[]{:S(2)}) copy-start(s32[48,4]{0,1:T(4,128)} %get-tuple-element.22) | copy-start | bytes 2308
  77.5 10.2 %collective-permute-start.6 = (f32[8,16,128]{2,1,0:T(8,128)S(1)}, f32[8,16,128]{2,1,0:T(8,128)S(1)}, u32[]{:S(2)}, u32[]{:S(2)}) collective-permute-start(f32[8,16,128]{2,1,0:T(8,128)S(1)} %get-tuple-element.5), channel_id=1, source_target_pairs={{0,16},{1,17},{2,18},{3,19},{4,20},{5,21},{6,22},{7,23},{8,24},{9,... | collective-permute-start | bytes 196616 | tf_op jit(solution)/shard_map/ppermute | solution.py:23
  80.9 6.3 %collective-permute-start.7 = (f32[8,16,128]{2,1,0:T(8,128)S(1)}, f32[8,16,128]{2,1,0:T(8,128)S(1)}, u32[]{:S(2)}, u32[]{:S(2)}) collective-permute-start(f32[8,16,128]{2,1,0:T(8,128)S(1)} %get-tuple-element.6), channel_id=1, source_target_pairs={{16,0},{17,1},{18,2},{19,3},{20,4},{21,5},{22,6},{23,7},{24,8},{25... | collective-permute-start | bytes 196616 | tf_op jit(solution)/shard_map/ppermute | solution.py:25
  89.1 1.2 copy-start
  95.9 10.0 %collective-permute-start.8 = (f32[48,16,128]{2,1,0:T(8,128)S(1)}, f32[48,16,128]{2,1,0:T(8,128)S(1)}, u32[]{:S(2)}, u32[]{:S(2)}) collective-permute-start(f32[48,16,128]{2,1,0:T(8,128)S(1)} %copy.74), channel_id=1, source_target_pairs={{0,1},{1,2},{2,3},{3,4},{4,5},{5,6},{6,7},{7,8},{8,9},{9,10},{10,1... | collective-permute-start | bytes 1179656 | tf_op jit(solution)/shard_map/ppermute | solution.py:12
  107.8 10.5 %collective-permute-start.9 = (f32[48,16,128]{2,1,0:T(8,128)S(1)}, f32[48,16,128]{2,1,0:T(8,128)S(1)}, u32[]{:S(2)}, u32[]{:S(2)}) collective-permute-start(f32[48,16,128]{2,1,0:T(8,128)S(1)} %copy.76), channel_id=1, source_target_pairs={{0,2},{1,3},{2,4},{3,5},{4,6},{5,7},{6,8},{7,9},{8,10},{9,11},{10,... | collective-permute-start | bytes 1179656 | tf_op jit(solution)/shard_map/ppermute | solution.py:12
  120.3 9.6 %collective-permute-start.10 = (f32[48,16,128]{2,1,0:T(8,128)S(1)}, f32[48,16,128]{2,1,0:T(8,128)S(1)}, u32[]{:S(2)}, u32[]{:S(2)}) collective-permute-start(f32[48,16,128]{2,1,0:T(8,128)S(1)} %copy.78), channel_id=1, source_target_pairs={{0,4},{1,5},{2,6},{3,7},{4,8},{5,9},{6,10},{7,11},{8,12},{9,13},{1... | collective-permute-start | bytes 1179656 | tf_op jit(solution)/shard_map/ppermute | solution.py:12
  131.9 16.2 %collective-permute-start.11 = (f32[48,16,128]{2,1,0:T(8,128)S(1)}, f32[48,16,128]{2,1,0:T(8,128)S(1)}, u32[]{:S(2)}, u32[]{:S(2)}) collective-permute-start(f32[48,16,128]{2,1,0:T(8,128)S(1)} %copy.80), channel_id=1, source_target_pairs={{0,8},{1,9},{2,10},{3,11},{4,12},{5,13},{6,14},{7,15},{8,0},{9,1},... | collective-permute-start | bytes 1179656 | tf_op jit(solution)/shard_map/ppermute | solution.py:12
  148.9 11.0 %copy-start.2 = (s32[48,16,128]{2,1,0:T(8,128)S(1)}, s32[48,16,128]{2,1,0:T(8,128)}, u32[]{:S(2)}) copy-start(s32[48,16,128]{2,1,0:T(8,128)} %copy-done.1) | copy-start | bytes 1179652
  148.9 11.0 %copy-start.4 = (s32[48,16,128]{2,1,0:T(8,128)S(1)}, s32[48,16,128]{2,1,0:T(8,128)}, u32[]{:S(2)}) copy-start(s32[48,16,128]{2,1,0:T(8,128)} %copy-done.3) | copy-start | bytes 1179652
  148.9 11.0 %copy-start.6 = (s32[48,16,128]{2,1,0:T(8,128)S(1)}, s32[48,16,128]{2,1,0:T(8,128)}, u32[]{:S(2)}) copy-start(s32[48,16,128]{2,1,0:T(8,128)} %copy-done.5) | copy-start | bytes 1179652
  149.4 5.4 %collective-permute-start.13 = (f32[48,16,128]{2,1,0:T(8,128)S(1)}, f32[48,16,128]{2,1,0:T(8,128)S(1)}, u32[]{:S(2)}, u32[]{:S(2)}) collective-permute-start(f32[48,16,128]{2,1,0:T(8,128)S(1)} %copy.82), channel_id=1, source_target_pairs={{1,0},{2,1},{3,2},{4,3},{5,4},{6,5},{7,6},{8,7},{9,8},{10,9},{11,1... | collective-permute-start | bytes 1179656 | tf_op jit(solution)/shard_map/ppermute | solution.py:25
  149.5 10.3 %collective-permute-start.12 = (f32[48,16,128]{2,1,0:T(8,128)S(1)}, f32[48,16,128]{2,1,0:T(8,128)S(1)}, u32[]{:S(2)}, u32[]{:S(2)}) collective-permute-start(f32[48,16,128]{2,1,0:T(8,128)S(1)} %copy.82), channel_id=1, source_target_pairs={{0,1},{1,2},{2,3},{3,4},{4,5},{5,6},{6,7},{7,8},{8,9},{9,10},{10,1... | collective-permute-start | bytes 1179656 | tf_op jit(solution)/shard_map/ppermute | solution.py:23
where the time goes:
time: 176 us
  waiting for transfers between devices  109 us (62%)
  other arithmetic  36 us (20%)
  local copies, waits for them, and re-layouts  17.9 us (10%)
  starting transfers between devices  7.4 us (4%)
  matrix products  5.06 us (3%)
    ppermute x8, waiting for transfers between devices, passed_along(): return lax.ppermute(value, axis, pairs)  86 us
    reduce_sum x2, other arithmetic, zonal_pass(): return jnp.sum(banded * extended[:, None, :, :], axis=2)  29.9 us
    ppermute x3, waiting for transfers between devices, extended_2(): lax.ppermute(head, axis, [((i + 1) % count, i) for i in range(ends)])  13 us
    ppermute x3, waiting for transfers between devices, extended_2(): lax.ppermute(tail, axis, [(i, (i + 1) % count) for i in range(ends)])  9.7 us
    dot_general x1, matrix products, meridional_pass(): return jnp.einsum(form, selector, extended, precision=lax.Precision.HIGHEST)  5.06 us
    ppermute x8, local copies, waits for them, and re-layouts, passed_along(): return lax.ppermute(value, axis, pairs)  4.47 us
    select_n x8, local copies, waits for them, and re-layouts, zonal_pass(): moved = jnp.where(taken[:, None, :], other, moved)  4.14 us
    ppermute x3, starting transfers between devices, extended_2(): lax.ppermute(tail, axis, [(i, (i + 1) % count) for i in range(ends)])  3.92 us
  transfers between devices with their start and end apart: 14, of which 13 were waited for; matrix products, arithmetic and copies ran while one was open for 5% of the time, Pallas kernels for 0%

commit v1 on v0

v1 whole, which is shorter than its diff:
```python
import functools
import math

import jax
import jax.numpy as jnp
from jax import lax
from jax.experimental import pallas as pl
from jax.experimental.pallas import tpu as pltpu
from jax.sharding import PartitionSpec as P

TMAX = 6
REACH = TMAX + 2
SUB = 8
PIECE = 16


def turned(parts, per):
    parts = list(parts)
    count = len(parts)
    lanes = parts[0].shape[1]
    block = lax.broadcasted_iota(jnp.int32, parts[0].shape, 1) // per
    bit = count // 2
    while bit:
        high = (block // bit) % 2 == 1
        move = per * bit
        for i in range(count):
            if i & bit:
                continue
            a, b = parts[i], parts[i | bit]
            parts[i] = jnp.where(high, pltpu.roll(b, move, 1), a)
            parts[i | bit] = jnp.where(high, b, pltpu.roll(a, lanes - move, 1))
        bit //= 2
    return parts


def circled(field, offset, weights, per):
    count, lanes = field.shape
    lane = lax.broadcasted_iota(jnp.int32, field.shape, 1)
    following = pltpu.roll(field, count - 1, 0)
    total = weights[0] * field
    for k in range(1, 4):
        mixed = jnp.where(lane >= per * k, field, following)
        total = total + weights[k] * pltpu.roll(mixed, lanes - per * k, 1)
    shift = ((offset + 1) * per + count * lanes) % (count * lanes)
    coarse, fine = shift // lanes, shift % lanes
    near = pltpu.roll(total, coarse, 0)
    far = pltpu.roll(near, 1, 0)
    return pltpu.roll(jnp.where(lane < lanes - fine, near, far), fine, 1)


def kernel(
    n, bands, groups, rows, piece, per, per_level,
    x_ref, lon_off, lon_w, lat_off, lat_w, out_ref,
    send, recv, first, back, home,
    send_sem, recv_sem, back_sem, home_sem, halo_send, halo_recv, own_sem,
):
    me = lax.axis_index("lon")
    split = n // groups
    group, share = me // split, me % split
    part = lax.axis_index("band") * split + share
    parts_all = bands * split
    level = group * per // per_level
    chunks = rows // piece
    tile_rows = math.gcd(SUB, piece)
    slot = send.shape[0] // n
    order = [0, chunks - 1] + list(range(1, chunks - 1)) if chunks > 1 else [0]

    barrier = pltpu.get_barrier_semaphore()

    def greet(d, carry):
        pl.semaphore_signal(
            barrier, inc=1, device_id={"lon": lax.rem(me + d, n)},
            device_id_type=pl.DeviceIdType.MESH,
        )
        return carry

    lax.fori_loop(1, n, greet, 0)

    def beside(step):
        other = lax.rem(part + step + parts_all, parts_all)
        return {"band": other // split, "lon": group * split + other % split}

    @pl.when(part > 0)
    def _():
        pl.semaphore_signal(
            barrier, inc=1, device_id=beside(-1), device_id_type=pl.DeviceIdType.MESH
        )

    @pl.when(part < parts_all - 1)
    def _():
        pl.semaphore_signal(
            barrier, inc=1, device_id=beside(1), device_id_type=pl.DeviceIdType.MESH
        )

    def place_of(peer, chunk):
        return pl.ds(pl.multiple_of(peer * slot + chunk * piece, SUB), piece)

    def pack(chunk):
        for s in range(split):

            def tile(t, carry):
                row = chunk * piece + t * tile_rows
                start = (s * rows + row) * groups
                parts = [
                    x_ref[pl.ds(start + i, tile_rows, stride=groups), :] for i in range(groups)
                ]
                for g, block in enumerate(turned(parts, per)):
                    to = (g * split + s) * slot + row
                    send[pl.ds(pl.multiple_of(to, tile_rows), tile_rows), :] = block
                return carry

            lax.fori_loop(0, piece // tile_rows, tile, 0)

    def across(source, target, s_sem, r_sem, chunk, d):
        peer = lax.rem(me + d, n)
        return pltpu.make_async_remote_copy(
            src_ref=source.at[place_of(peer, chunk), :],
            dst_ref=target.at[place_of(me, chunk), :],
            send_sem=s_sem.at[chunk, d],
            recv_sem=r_sem.at[chunk, d],
            device_id={"lon": peer},
            device_id_type=pl.DeviceIdType.MESH,
        )

    def own(source, target, chunk, which):
        place = place_of(me, chunk)
        return pltpu.make_async_copy(
            source.at[place, :], target.at[place, :], own_sem.at[which, chunk]
        )

    def start_all(source, target, s_sem, r_sem, chunk, which):
        def one(d, carry):
            across(source, target, s_sem, r_sem, chunk, d).start()
            return carry

        lax.fori_loop(1, n, one, 0)
        own(source, target, chunk, which).start()

    def wait_all(source, target, s_sem, r_sem, chunk, which):
        def one(d, carry):
            across(source, target, s_sem, r_sem, chunk, d).wait_recv()
            return carry

        lax.fori_loop(1, n, one, 0)
        own(source, target, chunk, which).wait()

    def wait_sent(source, target, s_sem, r_sem, chunk):
        def one(d, carry):
            across(source, target, s_sem, r_sem, chunk, d).wait_send()
            return carry

        lax.fori_loop(1, n, one, 0)

    forward = (send, recv, send_sem, recv_sem)
    backward = (back, home, back_sem, home_sem)

    pack(order[0])
    above = jnp.where(part > 0, 1, 0)
    below = jnp.where(part < parts_all - 1, 1, 0)
    pl.semaphore_wait(barrier, n - 1 + above + below)

    for place, chunk in enumerate(order):
        if place:
            pack(chunk)
        start_all(*forward, chunk, 0)

    @pl.when(part == 0)
    def _():
        first[pl.ds(0, REACH)] = jnp.zeros((REACH,) + first.shape[1:], jnp.float32)

    @pl.when(part == parts_all - 1)
    def _():
        first[pl.ds(REACH + rows, REACH)] = jnp.zeros((REACH,) + first.shape[1:], jnp.float32)

    up = pltpu.make_async_remote_copy(
        src_ref=first.at[pl.ds(REACH, REACH)],
        dst_ref=first.at[pl.ds(REACH + rows, REACH)],
        send_sem=halo_send.at[0], recv_sem=halo_recv.at[0],
        device_id=beside(-1),
        device_id_type=pl.DeviceIdType.MESH,
    )
    down = pltpu.make_async_remote_copy(
        src_ref=first.at[pl.ds(rows, REACH)],
        dst_ref=first.at[pl.ds(0, REACH)],
        send_sem=halo_send.at[1], recv_sem=halo_recv.at[1],
        device_id=beside(1),
        device_id_type=pl.DeviceIdType.MESH,
    )

    base = share * rows

    def lon_params(row):
        return lon_off[base + row, level], [lon_w[k, base + row, level] for k in range(4)]

    for place, chunk in enumerate(order):
        wait_all(*forward, chunk, 0)

        def along(t, carry):
            for u in range(tile_rows):
                row = chunk * piece + t * tile_rows + u
                field = recv[pl.ds(row, n, stride=slot), :]
                first[REACH + row] = circled(field, *lon_params(row), per)
            return carry

        lax.fori_loop(0, piece // tile_rows, along, 0)
        if place == min(1, len(order) - 1):

            @pl.when(part > 0)
            def _():
                up.start()

            @pl.when(part < parts_all - 1)
            def _():
                down.start()

    @pl.when(part > 0)
    def _():
        up.wait_send()
        down.wait_recv()

    @pl.when(part < parts_all - 1)
    def _():
        down.wait_send()
        up.wait_recv()

    first_row = part * rows
    for chunk in range(chunks):

        def both(t, carry):
            for u in range(tile_rows):
                row = chunk * piece + t * tile_rows + u
                shift = lat_off[base + row, level]
                field = None
                for k in range(4):
                    source = jnp.clip(first_row + row - shift + (k - 1), 0, parts_all * rows - 1)
                    term = lat_w[k, base + row, level] * first[source - first_row + REACH]
                    field = term if field is None else field + term
                back[pl.ds(row, n, stride=slot), :] = circled(field, *lon_params(row), per)
            return carry

        lax.fori_loop(0, piece // tile_rows, both, 0)
        start_all(*backward, chunk, 1)

    for chunk in range(chunks):
        wait_all(*backward, chunk, 1)

        for s in range(split):

            def unpack(t, carry):
                row = chunk * piece + t * tile_rows
                start = (s * rows + row) * groups
                parts = [
                    home[pl.ds(pl.multiple_of((g * split + s) * slot + row, tile_rows), tile_rows), :]
                    for g in range(groups)
                ]
                for i, block in enumerate(turned(parts, per)):
                    out_ref[pl.ds(start + i, tile_rows, stride=groups), :] = block
                return carry

            lax.fori_loop(0, piece // tile_rows, unpack, 0)

    for chunk in range(chunks):
        wait_sent(*forward, chunk)
        wait_sent(*backward, chunk)


def per_device(tracers, lon_offset, lon_weights, lat_offset, lat_weights):
    rows, width, columns = tracers.shape
    n, bands = lax.axis_size("lon"), lax.axis_size("band")
    groups = width
    per = columns // groups
    per_level = columns // lon_offset.shape[1]
    assert n % groups == 0 and rows % (n // groups) == 0 and per_level % per == 0
    share = rows // (n // groups)
    piece = PIECE if share % PIECE == 0 else share
    chunks = share // piece
    slot = -(-share // SUB) * SUB
    smem = pl.BlockSpec(memory_space=pltpu.SMEM)
    vmem = pl.BlockSpec(memory_space=pltpu.VMEM)
    flat = pltpu.VMEM((n * slot, columns), jnp.float32)
    sems = pltpu.SemaphoreType.DMA((chunks, n))
    out = pl.pallas_call(
        functools.partial(kernel, n, bands, groups, share, piece, per, per_level),
        out_shape=jax.ShapeDtypeStruct((rows * width, columns), jnp.float32),
        in_specs=[vmem, smem, smem, smem, smem],
        out_specs=vmem,
        scratch_shapes=[
            flat,
            flat,
            pltpu.VMEM((share + 2 * REACH, n, columns), jnp.float32),
            flat,
            flat,
            sems,
            sems,
            sems,
            sems,
            pltpu.SemaphoreType.DMA((2,)),
            pltpu.SemaphoreType.DMA((2,)),
            pltpu.SemaphoreType.DMA((2, chunks)),
        ],
        compiler_params=pltpu.CompilerParams(collective_id=0, has_side_effects=True),
    )(tracers.reshape(rows * width, columns), lon_offset, lon_weights, lat_offset, lat_weights)
    return out.reshape(rows, width, columns)


def solution(mesh):
    return jax.shard_map(
        per_device,
        mesh=mesh,
        in_specs=(
            P("band", "lon", None),
            P("band", None),
            P(None, "band", None),
            P("band", None),
            P(None, "band", None),
        ),
        out_specs=P("band", "lon", None),
        check_vma=False,
    )
```

time: 176 us -> 43.3 us (0.25)
  waiting for transfers between devices: 109 us -> 0 us
  Pallas kernels: 0 us -> 37.7 us
  other arithmetic: 36 us -> 0 us
  local copies, waits for them, and re-layouts: 17.9 us -> 5.37 us
  starting transfers between devices: 7.4 us -> 0 us
  matrix products: 5.06 us -> 0 us
    ppermute x14 -> x0, waiting for transfers between devices: 109 us -> none  [the longest x8 86 us: passed_along(): return lax.ppermute(value, axis, pairs)]
    pallas_call x0 -> x1, Pallas kernels: none -> 37.7 us  [per_device(): pl.pallas_call(functools.partial(kernel, n, bands, groups, share, piece,...]
    reduce_sum x2 -> x0, other arithmetic: 29.9 us -> none  [zonal_pass(): return jnp.sum(banded * extended[:, None, :, :], axis=2)]
    ppermute x14 -> x0, starting transfers between devices: 7.4 us -> none  [the longest x3 3.92 us: extended_2(): lax.ppermute(tail, axis, [(i, (i + 1) % count) for i in range(ends)])]
    ppermute x10 -> x0, local copies, waits for them, and re-layouts: 6.36 us -> none  [the longest x8 4.47 us: passed_along(): return lax.ppermute(value, axis, pairs)]
    dot_general x1 -> x0, matrix products: 5.06 us -> none  [meridional_pass(): return jnp.einsum(form, selector, extended, precision=lax.Precision.HIGHEST)]
    select_n x8 -> x0, local copies, waits for them, and re-layouts: 4.14 us -> none  [zonal_pass(): moved = jnp.where(taken[:, None, :], other, moved)]
    select_n x8 -> x0, other arithmetic: 3.48 us -> none  [zonal_pass(): moved = jnp.where(taken[:, None, :], other, moved)]
  transfers between devices with their start and end apart: 14 -> 0, of which waited for: 13 -> 0; matrix products, arithmetic and copies ran while one was open for 5% -> 0% of each run, Pallas kernels for 0% -> 0%
where the time goes in v1:
time: 43.3 us; the launch traced here: 43 us
  Pallas kernels  37.7 us (87%)
  local copies, waits for them, and re-layouts  5.37 us (12%)
    pallas_call x1, Pallas kernels, per_device(): pl.pallas_call(functools.partial(kernel, n, bands, groups, share, piece,...  37.7 us
    unnamed x11, local copies, waits for them, and re-layouts  5.37 us

profile of v1, /device:TPU:0, one launch (start us, length us, event | category | flops | bytes accessed | tf_op | source)
XLA Modules:
  0.0 43.0 jit_solution(18407046243733239147)
XLA Ops:
  0.0 0.0 copy-start.2
  0.0 1.4 %copy.6.lon_off = s32[48,4]{1,0:T(8,128)} copy(s32[48,4]{0,1:T(4,128)} %param.6) | data formatting | bytes 1536 | tf_op args[1]
  1.4 0.0 copy-done.2
  1.4 0.0 copy-start
  1.4 0.7 %copy.8.lat_off = s32[48,4]{1,0:T(8,128)} copy(s32[48,4]{0,1:T(4,128)S(1)} %copy-done.2) | data formatting | bytes 1536 | tf_op args[3]
  2.1 0.0 copy-done
  2.1 0.0 copy-start.1
  2.1 0.8 %copy.7.lon_w = f32[4,48,4]{2,1,0:T(8,128)} copy(f32[4,48,4]{1,2,0:T(4,128)S(1)} %copy-done) | data formatting | bytes 6144 | tf_op args[2]
  2.9 0.0 copy-done.1
  2.9 0.7 %copy.9.lat_w = f32[4,48,4]{2,1,0:T(8,128)} copy(f32[4,48,4]{1,2,0:T(4,128)S(1)} %copy-done.1) | data formatting | bytes 6144 | tf_op args[4]
  3.6 37.7 %shard_map.55 = f32[768,128]{1,0:T(8,128)} custom-call(f32[768,128]{1,0:T(8,128)} %bitcast.3, s32[48,4]{1,0:T(8,128)} %copy.6.lon_off, f32[4,48,4]{2,1,0:T(8,128)} %copy.7.lon_w, s32[48,4]{1,0:T(8,128)} %copy.8.lat_off, f32[4,48,4]{2,1,0:T(8,128)} %copy.9.lat_w), custom_call_target="tpu_custom_call" | custom-call | tf_op jit(solution)/shard_map/pallas_call | solution.py:282
  41.3 1.8 %copy.11 = f32[48,16,128]{2,1,0:T(8,128)} copy(f32[48,16,128]{2,1,0:T(8,128)} %bitcast.2) | data formatting | bytes 786432
Async XLA Ops:
  0.0 1.4 %copy-start.2 = (s32[48,4]{0,1:T(4,128)S(1)}, s32[48,4]{0,1:T(4,128)}, u32[]{:S(2)}) copy-start(s32[48,4]{0,1:T(4,128)} %param.8) | copy-start | bytes 2308
  1.4 0.7 %copy-start = (f32[4,48,4]{1,2,0:T(4,128)S(1)}, f32[4,48,4]{1,2,0:T(4,128)}, u32[]{:S(2)}) copy-start(f32[4,48,4]{1,2,0:T(4,128)} %param.7) | copy-start | bytes 9220
  2.1 0.8 %copy-start.1 = (f32[4,48,4]{1,2,0:T(4,128)S(1)}, f32[4,48,4]{1,2,0:T(4,128)}, u32[]{:S(2)}) copy-start(f32[4,48,4]{1,2,0:T(4,128)} %param.9) | copy-start | bytes 9220

commit v2 on v1

v2 whole, which is shorter than its diff:
```python
import functools
import math

import jax
import jax.numpy as jnp
from jax import lax
from jax.experimental import pallas as pl
from jax.experimental.pallas import tpu as pltpu
from jax.sharding import PartitionSpec as P

TMAX = 6
REACH = TMAX + 2
SUB = 8
PIECE = 16


def turned(parts, per):
    parts = list(parts)
    count = len(parts)
    lanes = parts[0].shape[1]
    block = lax.broadcasted_iota(jnp.int32, parts[0].shape, 1) // per
    bit = count // 2
    while bit:
        high = (block // bit) % 2 == 1
        move = per * bit
        for i in range(count):
            if i & bit:
                continue
            a, b = parts[i], parts[i | bit]
            parts[i] = jnp.where(high, pltpu.roll(b, move, 1), a)
            parts[i | bit] = jnp.where(high, b, pltpu.roll(a, lanes - move, 1))
        bit //= 2
    return parts


def circled(field, offset, weights, per):
    count, lanes = field.shape
    lane = lax.broadcasted_iota(jnp.int32, field.shape, 1)
    following = pltpu.roll(field, count - 1, 0)
    total = weights[0] * field
    for k in range(1, 4):
        mixed = jnp.where(lane >= per * k, field, following)
        total = total + weights[k] * pltpu.roll(mixed, lanes - per * k, 1)
    shift = ((offset + 1) * per + count * lanes) % (count * lanes)
    coarse, fine = shift // lanes, shift % lanes
    near = pltpu.roll(total, coarse, 0)
    far = pltpu.roll(near, 1, 0)
    return pltpu.roll(jnp.where(lane < lanes - fine, near, far), fine, 1)


def kernel(
    n, bands, groups, rows, piece, per, per_level,
    x_hbm, lon_off_hbm, lon_w_hbm, lat_off_hbm, lat_w_hbm, out_hbm,
    x_ref, lon_off, lon_w, lat_off, lat_w, out_ref,
    send, recv, first, back, home, halo,
    in_sem, out_sem, param_sem, send_sem, recv_sem, back_sem, home_sem, halo_send, halo_recv,
):
    me = lax.axis_index("lon")
    band = lax.axis_index("band")
    split = n // groups
    group, share = me // split, me % split
    part = band * split + share
    parts_all = bands * split
    level = group * per // per_level
    chunks = rows // piece
    tile_rows = math.gcd(SUB, piece)
    slot = send.shape[0] // n
    block = piece * groups
    forwards = band % 2 == 1
    base = share * rows

    def chunk_at(step):
        return jnp.where(forwards, step, chunks - 1 - step)

    def fetch(step, s):
        place = pl.ds(pl.multiple_of((s * rows + chunk_at(step) * piece) * groups, SUB), block)
        return pltpu.make_async_copy(x_hbm.at[place, :], x_ref.at[place, :], in_sem.at[step, s])

    def deliver(step, s):
        place = pl.ds(pl.multiple_of((s * rows + chunk_at(step) * piece) * groups, SUB), block)
        return pltpu.make_async_copy(out_ref.at[place, :], out_hbm.at[place, :], out_sem.at[step, s])

    for step in range(chunks):
        for s in range(split):
            fetch(step, s).start()
    params = [
        pltpu.make_async_copy(source, target, param_sem.at[i])
        for i, (source, target) in enumerate(
            ((lon_off_hbm, lon_off), (lon_w_hbm, lon_w), (lat_off_hbm, lat_off), (lat_w_hbm, lat_w))
        )
    ]
    for param in params:
        param.start()

    barrier = pltpu.get_barrier_semaphore()

    def greet(d, carry):
        pl.semaphore_signal(
            barrier, inc=1, device_id={"lon": lax.rem(me + d, n)},
            device_id_type=pl.DeviceIdType.MESH,
        )
        return carry

    lax.fori_loop(1, n, greet, 0)

    def beside(step):
        other = lax.rem(part + step + parts_all, parts_all)
        return {"band": other // split, "lon": group * split + other % split}

    @pl.when(part > 0)
    def _():
        pl.semaphore_signal(
            barrier, inc=1, device_id=beside(-1), device_id_type=pl.DeviceIdType.MESH
        )

    @pl.when(part < parts_all - 1)
    def _():
        pl.semaphore_signal(
            barrier, inc=1, device_id=beside(1), device_id_type=pl.DeviceIdType.MESH
        )

    def pack(step):
        for s in range(split):
            fetch(step, s).wait()

            def tile(t, carry):
                row = chunk_at(step) * piece + t * tile_rows
                start = (s * rows + row) * groups
                parts = [
                    x_ref[pl.ds(start + i, tile_rows, stride=groups), :] for i in range(groups)
                ]
                for g, part_block in enumerate(turned(parts, per)):
                    to = (g * split + s) * slot + row
                    send[pl.ds(pl.multiple_of(to, tile_rows), tile_rows), :] = part_block
                return carry

            lax.fori_loop(0, piece // tile_rows, tile, 0)

    def place_of(peer, step):
        return pl.ds(pl.multiple_of(peer * slot + chunk_at(step) * piece, SUB), piece)

    def start_all(source, target, s_sem, r_sem, step):
        def one(d, carry):
            peer = lax.rem(me + d, n)
            pltpu.make_async_remote_copy(
                src_ref=source.at[place_of(peer, step), :],
                dst_ref=target.at[place_of(me, step), :],
                send_sem=s_sem,
                recv_sem=r_sem.at[step],
                device_id={"lon": peer},
                device_id_type=pl.DeviceIdType.MESH,
            ).start()
            return carry

        place = place_of(me, step)
        pltpu.make_async_copy(source.at[place, :], target.at[place, :], r_sem.at[step]).start()
        lax.fori_loop(1, n, one, 0)

    def wait_bytes(ref, sem, count):
        whole = ref.at[pl.ds(0, count), :]
        pltpu.make_async_copy(whole, whole, sem).wait()

    forward = (send, recv, send_sem, recv_sem)
    backward = (back, home, back_sem, home_sem)

    pack(0)
    above = jnp.where(part > 0, 1, 0)
    below = jnp.where(part < parts_all - 1, 1, 0)
    pl.semaphore_wait(barrier, n - 1 + above + below)
    start_all(*forward, 0)
    for step in range(1, chunks):
        pack(step)
        start_all(*forward, step)

    for param in params:
        param.wait()

    up = pltpu.make_async_remote_copy(
        src_ref=first.at[pl.ds(REACH, REACH)],
        dst_ref=halo.at[1],
        send_sem=halo_send.at[0], recv_sem=halo_recv.at[1],
        device_id=beside(-1),
        device_id_type=pl.DeviceIdType.MESH,
    )
    down = pltpu.make_async_remote_copy(
        src_ref=first.at[pl.ds(rows, REACH)],
        dst_ref=halo.at[0],
        send_sem=halo_send.at[1], recv_sem=halo_recv.at[0],
        device_id=beside(1),
        device_id_type=pl.DeviceIdType.MESH,
    )
    has_up, has_down = part > 0, part < parts_all - 1

    def send_edges(low, high):
        @pl.when(jnp.logical_and(low, has_up))
        def _():
            up.start()

        @pl.when(jnp.logical_and(high, has_down))
        def _():
            down.start()

    def take_edges(low, high):
        @pl.when(jnp.logical_and(low, has_up))
        def _():
            down.wait_recv()
            first[pl.ds(0, REACH)] = halo[0]

        @pl.when(jnp.logical_and(high, has_down))
        def _():
            up.wait_recv()
            first[pl.ds(REACH + rows, REACH)] = halo[1]

    backwards = jnp.logical_not(forwards)

    def lon_params(row):
        return lon_off[level, base + row], [lon_w[k, level, base + row] for k in range(4)]

    def along(step):
        def some(t, carry):
            for u in range(tile_rows):
                row = chunk_at(step) * piece + t * tile_rows + u
                field = recv[pl.ds(row, n, stride=slot), :]
                first[REACH + row] = circled(field, *lon_params(row), per)
            return carry

        lax.fori_loop(0, piece // tile_rows, some, 0)

    first_row = part * rows

    def across_and_along(step):
        def some(t, carry):
            for u in range(tile_rows):
                row = chunk_at(step) * piece + t * tile_rows + u
                shift = lat_off[level, base + row]
                field = None
                for k in range(4):
                    source = jnp.clip(first_row + row - shift + (k - 1), 0, parts_all * rows - 1)
                    term = lat_w[k, level, base + row] * first[source - first_row + REACH]
                    field = term if field is None else field + term
                back[pl.ds(row, n, stride=slot), :] = circled(field, *lon_params(row), per)
            return carry

        lax.fori_loop(0, piece // tile_rows, some, 0)

    for step in range(chunks):
        wait_bytes(recv, recv_sem.at[step], n * piece)
        along(step)
        if chunks == 1:
            send_edges(True, True)
        elif step == 0:
            send_edges(forwards, backwards)
        elif step == chunks - 1:
            send_edges(backwards, forwards)
        if step:
            if step == 1:
                take_edges(forwards, backwards)
            across_and_along(step - 1)
            start_all(*backward, step - 1)
    if chunks == 1:
        take_edges(True, True)
    else:
        take_edges(backwards, forwards)
    across_and_along(chunks - 1)
    start_all(*backward, chunks - 1)

    for step in range(chunks):
        wait_bytes(home, home_sem.at[step], n * piece)
        for s in range(split):

            def unpack(t, carry):
                row = chunk_at(step) * piece + t * tile_rows
                start = (s * rows + row) * groups
                parts = [
                    home[pl.ds(pl.multiple_of((g * split + s) * slot + row, tile_rows), tile_rows), :]
                    for g in range(groups)
                ]
                for i, part_block in enumerate(turned(parts, per)):
                    out_ref[pl.ds(start + i, tile_rows, stride=groups), :] = part_block
                return carry

            lax.fori_loop(0, piece // tile_rows, unpack, 0)
            deliver(step, s).start()

    wait_bytes(send, send_sem, (n - 1) * rows)
    wait_bytes(back, back_sem, (n - 1) * rows)

    @pl.when(has_up)
    def _():
        up.wait_send()

    @pl.when(has_down)
    def _():
        down.wait_send()

    for step in range(chunks):
        for s in range(split):
            deliver(step, s).wait()


def per_device(tracers, lon_offset, lon_weights, lat_offset, lat_weights):
    rows, width, columns = tracers.shape
    n, bands = lax.axis_size("lon"), lax.axis_size("band")
    groups = width
    per = columns // groups
    levels = lon_offset.shape[1]
    per_level = columns // levels
    split = n // groups
    assert n % groups == 0 and rows % split == 0 and per_level % per == 0
    share = rows // split
    piece = PIECE if share % PIECE == 0 else share
    chunks = share // piece
    slot = -(-share // SUB) * SUB
    flat = pltpu.VMEM((n * slot, columns), jnp.float32)
    whole = pltpu.VMEM((rows * width, columns), jnp.float32)
    dma = pltpu.SemaphoreType.DMA
    out = pl.pallas_call(
        functools.partial(kernel, n, bands, groups, share, piece, per, per_level),
        out_shape=jax.ShapeDtypeStruct((rows * width, columns), jnp.float32),
        in_specs=[pl.BlockSpec(memory_space=pl.ANY)] * 5,
        out_specs=pl.BlockSpec(memory_space=pl.ANY),
        scratch_shapes=[
            whole,
            pltpu.SMEM((levels, rows), jnp.int32),
            pltpu.SMEM((4, levels, rows), jnp.float32),
            pltpu.SMEM((levels, rows), jnp.int32),
            pltpu.SMEM((4, levels, rows), jnp.float32),
            whole,
            flat,
            flat,
            pltpu.VMEM((share + 2 * REACH, n, columns), jnp.float32),
            flat,
            flat,
            pltpu.VMEM((2, REACH, n, columns), jnp.float32),
            dma((chunks, split)),
            dma((chunks, split)),
            dma((4,)),
            dma,
            dma((chunks,)),
            dma,
            dma((chunks,)),
            dma((2,)),
            dma((2,)),
        ],
        compiler_params=pltpu.CompilerParams(collective_id=0, has_side_effects=True),
    )(
        tracers.reshape(rows * width, columns),
        lon_offset.T,
        lon_weights.transpose(0, 2, 1),
        lat_offset.T,
        lat_weights.transpose(0, 2, 1),
    )
    return out.reshape(rows, width, columns)


def solution(mesh):
    return jax.shard_map(
        per_device,
        mesh=mesh,
        in_specs=(
            P("band", "lon", None),
            P("band", None),
            P(None, "band", None),
            P("band", None),
            P(None, "band", None),
        ),
        out_specs=P("band", "lon", None),
        check_vma=False,
    )
```

time: 43.3 us -> 29.2 us (0.67)
  Pallas kernels: 37.7 us -> 27.3 us
  local copies, waits for them, and re-layouts: 5.37 us -> 1.77 us
    pallas_call x1, Pallas kernels: 37.7 us -> 27.3 us  [per_device(): pl.pallas_call(functools.partial(kernel, n, bands, groups, share, piece,...]
    unnamed x11 -> x1, local copies, waits for them, and re-layouts: 5.37 us -> 1.77 us
where the time goes in v2:
time: 29.2 us; the launch traced here: 29 us
  Pallas kernels  27.3 us (93%)
  local copies, waits for them, and re-layouts  1.77 us (6%)
    pallas_call x1, Pallas kernels, per_device(): pl.pallas_call(functools.partial(kernel, n, bands, groups, share, piece,...  27.3 us
    unnamed x1, local copies, waits for them, and re-layouts  1.77 us

profile of v2, /device:TPU:0, one launch (start us, length us, event | category | flops | bytes accessed | tf_op | source)
XLA Modules:
  0.0 29.0 jit_solution(17527067906924504809)
XLA Ops:
  0.0 27.3 %shard_map.55 = f32[768,128]{1,0:T(8,128)} custom-call(f32[768,128]{1,0:T(8,128)} %bitcast.7, s32[4,48]{1,0:T(4,128)} %bitcast.10, f32[4,4,48]{2,1,0:T(4,128)} %bitcast.8, s32[4,48]{1,0:T(4,128)} %bitcast.11, f32[4,4,48]{2,1,0:T(4,128)} %bitcast.9), custom_call_target="tpu_custom_call" | custom-call | tf_op jit(solution)/shard_map/pallas_call | solution.py:317
  27.3 1.8 %copy.7 = f32[48,16,128]{2,1,0:T(8,128)} copy(f32[48,16,128]{2,1,0:T(8,128)} %bitcast.6) | data formatting | bytes 786432

commit v3 on v2

--- a/solution.py
+++ b/solution.py
@@ -50,10 +50,10 @@
 
 def kernel(
     n, bands, groups, rows, piece, per, per_level,
-    x_hbm, lon_off_hbm, lon_w_hbm, lat_off_hbm, lat_w_hbm, out_hbm,
-    x_ref, lon_off, lon_w, lat_off, lat_w, out_ref,
+    x_hbm, lon_off_hbm, lon_w_hbm, lat_off_hbm, lat_w_hbm, out_ref,
+    x_ref, lon_off, lon_w, lat_off, lat_w,
     send, recv, first, back, home, halo,
-    in_sem, out_sem, param_sem, send_sem, recv_sem, back_sem, home_sem, halo_send, halo_recv,
+    in_sem, param_sem, send_sem, recv_sem, back_sem, home_sem, halo_send, halo_recv,
 ):
     me = lax.axis_index("lon")
     band = lax.axis_index("band")
@@ -76,10 +76,6 @@
         place = pl.ds(pl.multiple_of((s * rows + chunk_at(step) * piece) * groups, SUB), block)
         return pltpu.make_async_copy(x_hbm.at[place, :], x_ref.at[place, :], in_sem.at[step, s])
 
-    def deliver(step, s):
-        place = pl.ds(pl.multiple_of((s * rows + chunk_at(step) * piece) * groups, SUB), block)
-        return pltpu.make_async_copy(out_ref.at[place, :], out_hbm.at[place, :], out_sem.at[step, s])
-
     for step in range(chunks):
         for s in range(split):
             fetch(step, s).start()
@@ -140,8 +136,8 @@
         return pl.ds(pl.multiple_of(peer * slot + chunk_at(step) * piece, SUB), piece)
 
     def start_all(source, target, s_sem, r_sem, step):
-        def one(d, carry):
-            peer = lax.rem(me + d, n)
+        def one(i, carry):
+            peer = lax.rem(me + i // 2 + jnp.where(i % 2 == 0, n // 2, 1), n)
             pltpu.make_async_remote_copy(
                 src_ref=source.at[place_of(peer, step), :],
                 dst_ref=target.at[place_of(me, step), :],
@@ -154,7 +150,7 @@
 
         place = place_of(me, step)
         pltpu.make_async_copy(source.at[place, :], target.at[place, :], r_sem.at[step]).start()
-        lax.fori_loop(1, n, one, 0)
+        lax.fori_loop(0, n - 1, one, 0)
 
     def wait_bytes(ref, sem, count):
         whole = ref.at[pl.ds(0, count), :]
@@ -280,7 +276,6 @@
                 return carry
 
             lax.fori_loop(0, piece // tile_rows, unpack, 0)
-            deliver(step, s).start()
 
     wait_bytes(send, send_sem, (n - 1) * rows)
     wait_bytes(back, back_sem, (n - 1) * rows)
@@ -292,10 +287,6 @@
     @pl.when(has_down)
     def _():
         down.wait_send()
-
-    for step in range(chunks):
-        for s in range(split):
-            deliver(step, s).wait()
 
 
 def per_device(tracers, lon_offset, lon_weights, lat_offset, lat_weights):
@@ -316,23 +307,21 @@
     dma = pltpu.SemaphoreType.DMA
     out = pl.pallas_call(
         functools.partial(kernel, n, bands, groups, share, piece, per, per_level),
-        out_shape=jax.ShapeDtypeStruct((rows * width, columns), jnp.float32),
+        out_shape=whole,
         in_specs=[pl.BlockSpec(memory_space=pl.ANY)] * 5,
-        out_specs=pl.BlockSpec(memory_space=pl.ANY),
+        out_specs=pl.BlockSpec(memory_space=pltpu.VMEM),
         scratch_shapes=[
             whole,
             pltpu.SMEM((levels, rows), jnp.int32),
             pltpu.SMEM((4, levels, rows), jnp.float32),
             pltpu.SMEM((levels, rows), jnp.int32),
             pltpu.SMEM((4, levels, rows), jnp.float32),
-            whole,
             flat,
             flat,
             pltpu.VMEM((share + 2 * REACH, n, columns), jnp.float32),
             flat,
             flat,
             pltpu.VMEM((2, REACH, n, columns), jnp.float32),
-            dma((chunks, split)),
             dma((chunks, split)),
             dma((4,)),
             dma,

time: 29.2 us -> 29.6 us (1.014)
  Pallas kernels: 27.3 us -> 28.7 us
  local copies, waits for them, and re-layouts: 1.77 us -> 0.75 us
    pallas_call x1, Pallas kernels: 27.3 us -> 28.7 us  [per_device(): pl.pallas_call(functools.partial(kernel, n, bands, groups, share, piece,...]
    unnamed x1, local copies, waits for them, and re-layouts: 1.77 us -> 0.75 us
where the time goes in v3:
time: 29.6 us; the launch traced here: 29.5 us
  Pallas kernels  28.7 us (97%)
  local copies, waits for them, and re-layouts  0.75 us (3%)
    pallas_call x1, Pallas kernels, per_device(): pl.pallas_call(functools.partial(kernel, n, bands, groups, share, piece,...  28.7 us
    unnamed x1, local copies, waits for them, and re-layouts  0.75 us

profile of v3, /device:TPU:0, one launch (start us, length us, event | category | flops | bytes accessed | tf_op | source)
XLA Modules:
  0.0 29.5 jit_solution(2823291863222554191)
XLA Ops:
  0.0 28.7 %shard_map.55 = f32[768,128]{1,0:T(8,128)S(1)} custom-call(f32[768,128]{1,0:T(8,128)} %bitcast.7, s32[4,48]{1,0:T(4,128)} %bitcast.10, f32[4,4,48]{2,1,0:T(4,128)} %bitcast.8, s32[4,48]{1,0:T(4,128)} %bitcast.11, f32[4,4,48]{2,1,0:T(4,128)} %bitcast.9), custom_call_target="tpu_custom_call" | custom-call | tf_op jit(solution)/shard_map/pallas_call | solution.py:308
  28.8 0.7 %copy.7 = f32[48,16,128]{2,1,0:T(8,128)} copy(f32[48,16,128]{2,1,0:T(8,128)S(1)} %bitcast.6) | data formatting | bytes 786432

commit v4 on v3

--- a/solution.py
+++ b/solution.py
@@ -11,7 +11,7 @@
 TMAX = 6
 REACH = TMAX + 2
 SUB = 8
-PIECE = 16
+PIECE = 8
 
 
 def turned(parts, per):

time: 29.6 us -> 26.9 us (0.909)
  Pallas kernels: 28.7 us -> 26 us
    pallas_call x1, Pallas kernels: 28.7 us -> 26 us  [per_device(): pl.pallas_call(functools.partial(kernel, n, bands, groups, share, piece,...]
where the time goes in v4:
time: 26.9 us; the launch traced here: 26.8 us
  Pallas kernels  26 us (97%)
  local copies, waits for them, and re-layouts  0.75 us (3%)
    pallas_call x1, Pallas kernels, per_device(): pl.pallas_call(functools.partial(kernel, n, bands, groups, share, piece,...  26 us
    unnamed x1, local copies, waits for them, and re-layouts  0.75 us

profile of v4, /device:TPU:0, one launch (start us, length us, event | category | flops | bytes accessed | tf_op | source)
XLA Modules:
  0.0 26.8 jit_solution(1081376962680766595)
XLA Ops:
  0.0 26.0 %shard_map.55 = f32[768,128]{1,0:T(8,128)S(1)} custom-call(f32[768,128]{1,0:T(8,128)} %bitcast.7, s32[4,48]{1,0:T(4,128)} %bitcast.10, f32[4,4,48]{2,1,0:T(4,128)} %bitcast.8, s32[4,48]{1,0:T(4,128)} %bitcast.11, f32[4,4,48]{2,1,0:T(4,128)} %bitcast.9), custom_call_target="tpu_custom_call" | custom-call | tf_op jit(solution)/shard_map/pallas_call | solution.py:308
  26.0 0.7 %copy.7 = f32[48,16,128]{2,1,0:T(8,128)} copy(f32[48,16,128]{2,1,0:T(8,128)S(1)} %bitcast.6) | data formatting | bytes 786432

commit v5 on v4

--- a/solution.py
+++ b/solution.py
@@ -33,26 +33,34 @@
     return parts
 
 
-def circled(field, offset, weights, per):
-    count, lanes = field.shape
-    lane = lax.broadcasted_iota(jnp.int32, field.shape, 1)
-    following = pltpu.roll(field, count - 1, 0)
-    total = weights[0] * field
-    for k in range(1, 4):
-        mixed = jnp.where(lane >= per * k, field, following)
-        total = total + weights[k] * pltpu.roll(mixed, lanes - per * k, 1)
-    shift = ((offset + 1) * per + count * lanes) % (count * lanes)
-    coarse, fine = shift // lanes, shift % lanes
-    near = pltpu.roll(total, coarse, 0)
-    far = pltpu.roll(near, 1, 0)
-    return pltpu.roll(jnp.where(lane < lanes - fine, near, far), fine, 1)
+def circled(fields, followings, offsets, weights, per, spin):
+    count, lanes = fields[0].shape
+    lane = lax.broadcasted_iota(jnp.int32, fields[0].shape, 1)
+    turns = []
+    for u, (field, following) in enumerate(zip(fields, followings)):
+        total = weights[u][0] * field
+        for k in range(1, 4):
+            mixed = jnp.where(lane >= per * k, field, following)
+            total = total + weights[u][k] * pltpu.roll(mixed, lanes - per * k, 1)
+        shift = ((offsets[u] + 1) * per + count * lanes) % (count * lanes)
+        coarse, fine = shift // lanes, shift % lanes
+        total = pltpu.roll(total, fine, 1)
+        spin[pl.ds(2 * u * count, count), :] = total
+        spin[pl.ds((2 * u + 1) * count, count), :] = total
+        turns.append((coarse, fine))
+    results = []
+    for u, (coarse, fine) in enumerate(turns):
+        near = spin[pl.ds((2 * u + 1) * count - coarse, count), :]
+        far = spin[pl.ds((2 * u + 1) * count - 1 - coarse, count), :]
+        results.append(jnp.where(lane >= fine, near, far))
+    return results
 
 
 def kernel(
     n, bands, groups, rows, piece, per, per_level,
     x_hbm, lon_off_hbm, lon_w_hbm, lat_off_hbm, lat_w_hbm, out_ref,
     x_ref, lon_off, lon_w, lat_off, lat_w,
-    send, recv, first, back, home, halo,
+    send, recv, first, back, home, halo, spin,
     in_sem, param_sem, send_sem, recv_sem, back_sem, home_sem, halo_send, halo_recv,
 ):
     me = lax.axis_index("lon")
@@ -209,15 +217,21 @@
 
     backwards = jnp.logical_not(forwards)
 
-    def lon_params(row):
-        return lon_off[level, base + row], [lon_w[k, level, base + row] for k in range(4)]
+    def turned_rows(places, fields, followings):
+        offsets = [lon_off[level, base + row] for row in places]
+        weights = [[lon_w[k, level, base + row] for k in range(4)] for row in places]
+        return circled(fields, followings, offsets, weights, per, spin)
 
     def along(step):
         def some(t, carry):
-            for u in range(tile_rows):
-                row = chunk_at(step) * piece + t * tile_rows + u
-                field = recv[pl.ds(row, n, stride=slot), :]
-                first[REACH + row] = circled(field, *lon_params(row), per)
+            start = chunk_at(step) * piece + t * tile_rows
+            places = [start + u for u in range(tile_rows)]
+            tile = pl.multiple_of(start, tile_rows)
+            recv[pl.ds(n * slot + tile, tile_rows), :] = recv[pl.ds(tile, tile_rows), :]
+            fields = [recv[pl.ds(row, n, stride=slot), :] for row in places]
+            followings = [recv[pl.ds(slot + row, n, stride=slot), :] for row in places]
+            for row, result in zip(places, turned_rows(places, fields, followings)):
+                first[REACH + row] = result
             return carry
 
         lax.fori_loop(0, piece // tile_rows, some, 0)
@@ -226,15 +240,20 @@
 
     def across_and_along(step):
         def some(t, carry):
-            for u in range(tile_rows):
-                row = chunk_at(step) * piece + t * tile_rows + u
+            start = chunk_at(step) * piece + t * tile_rows
+            places = [start + u for u in range(tile_rows)]
+            fields = []
+            for row in places:
                 shift = lat_off[level, base + row]
                 field = None
                 for k in range(4):
                     source = jnp.clip(first_row + row - shift + (k - 1), 0, parts_all * rows - 1)
                     term = lat_w[k, level, base + row] * first[source - first_row + REACH]
                     field = term if field is None else field + term
-                back[pl.ds(row, n, stride=slot), :] = circled(field, *lon_params(row), per)
+                fields.append(field)
+            followings = [pltpu.roll(field, n - 1, 0) for field in fields]
+            for row, result in zip(places, turned_rows(places, fields, followings)):
+                back[pl.ds(row, n, stride=slot), :] = result
             return carry
 
         lax.fori_loop(0, piece // tile_rows, some, 0)
@@ -317,11 +336,12 @@
             pltpu.SMEM((levels, rows), jnp.int32),
             pltpu.SMEM((4, levels, rows), jnp.float32),
             flat,
-            flat,
+            pltpu.VMEM(((n + 1) * slot, columns), jnp.float32),
             pltpu.VMEM((share + 2 * REACH, n, columns), jnp.float32),
             flat,
             flat,
             pltpu.VMEM((2, REACH, n, columns), jnp.float32),
+            pltpu.VMEM((SUB * 2 * n, columns), jnp.float32),
             dma((chunks, split)),
             dma((4,)),
             dma,

time: 26.9 us -> 27 us (level)
  no operation moved by 1% of the time
where the time goes in v5:
time: 27 us; the launch traced here: 26.8 us
  Pallas kernels  26 us (96%)
  local copies, waits for them, and re-layouts  0.75 us (3%)
    pallas_call x1, Pallas kernels, per_device(): pl.pallas_call(functools.partial(kernel, n, bands, groups, share, piece,...  26 us
    unnamed x1, local copies, waits for them, and re-layouts  0.75 us

profile of v5, /device:TPU:0, one launch (start us, length us, event | category | flops | bytes accessed | tf_op | source)
XLA Modules:
  0.0 26.8 jit_solution(11644562127684183030)
XLA Ops:
  0.0 26.0 %shard_map.55 = f32[768,128]{1,0:T(8,128)S(1)} custom-call(f32[768,128]{1,0:T(8,128)} %bitcast.7, s32[4,48]{1,0:T(4,128)} %bitcast.10, f32[4,4,48]{2,1,0:T(4,128)} %bitcast.8, s32[4,48]{1,0:T(4,128)} %bitcast.11, f32[4,4,48]{2,1,0:T(4,128)} %bitcast.9), custom_call_target="tpu_custom_call" | custom-call | tf_op jit(solution)/shard_map/pallas_call | solution.py:327
  26.1 0.7 %copy.7 = f32[48,16,128]{2,1,0:T(8,128)} copy(f32[48,16,128]{2,1,0:T(8,128)S(1)} %bitcast.6) | data formatting | bytes 786432

commit v6 on v5

--- a/solution.py
+++ b/solution.py
@@ -74,28 +74,25 @@
     tile_rows = math.gcd(SUB, piece)
     slot = send.shape[0] // n
     block = piece * groups
-    forwards = band % 2 == 1
+    mirrored = band % 2 == 1
+    arrivals = [chunks - 1] + list(range(chunks - 1))
     base = share * rows
 
     def chunk_at(step):
-        return jnp.where(forwards, step, chunks - 1 - step)
+        return jnp.where(mirrored, chunks - 1 - step, step)
 
     def fetch(step, s):
         place = pl.ds(pl.multiple_of((s * rows + chunk_at(step) * piece) * groups, SUB), block)
         return pltpu.make_async_copy(x_hbm.at[place, :], x_ref.at[place, :], in_sem.at[step, s])
 
-    for step in range(chunks):
-        for s in range(split):
-            fetch(step, s).start()
+    for s in range(split):
+        fetch(arrivals[0], s).start()
     params = [
         pltpu.make_async_copy(source, target, param_sem.at[i])
         for i, (source, target) in enumerate(
             ((lon_off_hbm, lon_off), (lon_w_hbm, lon_w), (lat_off_hbm, lat_off), (lat_w_hbm, lat_w))
         )
     ]
-    for param in params:
-        param.start()
-
     barrier = pltpu.get_barrier_semaphore()
 
     def greet(d, carry):
@@ -122,6 +119,12 @@
         pl.semaphore_signal(
             barrier, inc=1, device_id=beside(1), device_id_type=pl.DeviceIdType.MESH
         )
+
+    for step in arrivals[1:]:
+        for s in range(split):
+            fetch(step, s).start()
+    for param in params:
+        param.start()
 
     def pack(step):
         for s in range(split):
@@ -167,12 +170,12 @@
     forward = (send, recv, send_sem, recv_sem)
     backward = (back, home, back_sem, home_sem)
 
-    pack(0)
+    pack(arrivals[0])
     above = jnp.where(part > 0, 1, 0)
     below = jnp.where(part < parts_all - 1, 1, 0)
     pl.semaphore_wait(barrier, n - 1 + above + below)
-    start_all(*forward, 0)
-    for step in range(1, chunks):
+    start_all(*forward, arrivals[0])
+    for step in arrivals[1:]:
         pack(step)
         start_all(*forward, step)
 
@@ -215,7 +218,7 @@
             up.wait_recv()
             first[pl.ds(REACH + rows, REACH)] = halo[1]
 
-    backwards = jnp.logical_not(forwards)
+    plain = jnp.logical_not(mirrored)
 
     def turned_rows(places, fields, followings):
         offsets = [lon_off[level, base + row] for row in places]
@@ -258,24 +261,24 @@
 
         lax.fori_loop(0, piece // tile_rows, some, 0)
 
-    for step in range(chunks):
+    for place, step in enumerate(arrivals):
         wait_bytes(recv, recv_sem.at[step], n * piece)
         along(step)
-        if chunks == 1:
-            send_edges(True, True)
-        elif step == 0:
-            send_edges(forwards, backwards)
-        elif step == chunks - 1:
-            send_edges(backwards, forwards)
-        if step:
+        if step == chunks - 1:
+            send_edges(mirrored, plain)
+        if step == 0:
+            send_edges(plain, mirrored)
+        if place >= 2:
             if step == 1:
-                take_edges(forwards, backwards)
+                take_edges(plain, mirrored)
             across_and_along(step - 1)
             start_all(*backward, step - 1)
-    if chunks == 1:
-        take_edges(True, True)
-    else:
-        take_edges(backwards, forwards)
+    if chunks < 3:
+        take_edges(plain, mirrored)
+    if chunks > 1:
+        across_and_along(chunks - 2)
+        start_all(*backward, chunks - 2)
+    take_edges(mirrored, plain)
     across_and_along(chunks - 1)
     start_all(*backward, chunks - 1)
 

time: 27 us -> 27.4 us (1.015)
  Pallas kernels: 26 us -> 26.5 us
    pallas_call x1, Pallas kernels: 26 us -> 26.5 us  [per_device(): pl.pallas_call(functools.partial(kernel, n, bands, groups, share, piece,...]
where the time goes in v6:
time: 27.4 us; the launch traced here: 27.3 us
  Pallas kernels  26.5 us (97%)
  local copies, waits for them, and re-layouts  0.75 us (3%)
    pallas_call x1, Pallas kernels, per_device(): pl.pallas_call(functools.partial(kernel, n, bands, groups, share, piece,...  26.5 us
    unnamed x1, local copies, waits for them, and re-layouts  0.75 us

profile of v6, /device:TPU:0, one launch (start us, length us, event | category | flops | bytes accessed | tf_op | source)
XLA Modules:
  0.0 27.3 jit_solution(6589658426502009976)
XLA Ops:
  0.0 26.5 %shard_map.55 = f32[768,128]{1,0:T(8,128)S(1)} custom-call(f32[768,128]{1,0:T(8,128)} %bitcast.7, s32[4,48]{1,0:T(4,128)} %bitcast.10, f32[4,4,48]{2,1,0:T(4,128)} %bitcast.8, s32[4,48]{1,0:T(4,128)} %bitcast.11, f32[4,4,48]{2,1,0:T(4,128)} %bitcast.9), custom_call_target="tpu_custom_call" | custom-call | tf_op jit(solution)/shard_map/pallas_call | solution.py:330
  26.5 0.7 %copy.7 = f32[48,16,128]{2,1,0:T(8,128)} copy(f32[48,16,128]{2,1,0:T(8,128)S(1)} %bitcast.6) | data formatting | bytes 786432

commit v7 on v6

--- a/solution.py
+++ b/solution.py
@@ -12,6 +12,7 @@
 REACH = TMAX + 2
 SUB = 8
 PIECE = 8
+AHEAD = 3
 
 
 def turned(parts, per):
@@ -175,9 +176,10 @@
     below = jnp.where(part < parts_all - 1, 1, 0)
     pl.semaphore_wait(barrier, n - 1 + above + below)
     start_all(*forward, arrivals[0])
-    for step in arrivals[1:]:
+    for place, step in enumerate(arrivals[1:], 1):
         pack(step)
-        start_all(*forward, step)
+        if place < AHEAD:
+            start_all(*forward, step)
 
     for param in params:
         param.wait()
@@ -263,6 +265,8 @@
 
     for place, step in enumerate(arrivals):
         wait_bytes(recv, recv_sem.at[step], n * piece)
+        if place + AHEAD < chunks:
+            start_all(*forward, arrivals[place + AHEAD])
         along(step)
         if step == chunks - 1:
             send_edges(mirrored, plain)

time: 27.4 us -> 27.5 us (level)
  no operation moved by 1% of the time
where the time goes in v7:
time: 27.5 us; the launch traced here: 27.3 us
  Pallas kernels  26.6 us (97%)
  local copies, waits for them, and re-layouts  0.75 us (3%)
    pallas_call x1, Pallas kernels, per_device(): pl.pallas_call(functools.partial(kernel, n, bands, groups, share, piece,...  26.6 us
    unnamed x1, local copies, waits for them, and re-layouts  0.75 us

profile of v7, /device:TPU:0, one launch (start us, length us, event | category | flops | bytes accessed | tf_op | source)
XLA Modules:
  0.0 27.3 jit_solution(11151070553491770721)
XLA Ops:
  0.0 26.6 %shard_map.55 = f32[768,128]{1,0:T(8,128)S(1)} custom-call(f32[768,128]{1,0:T(8,128)} %bitcast.7, s32[4,48]{1,0:T(4,128)} %bitcast.10, f32[4,4,48]{2,1,0:T(4,128)} %bitcast.8, s32[4,48]{1,0:T(4,128)} %bitcast.11, f32[4,4,48]{2,1,0:T(4,128)} %bitcast.9), custom_call_target="tpu_custom_call" | custom-call | tf_op jit(solution)/shard_map/pallas_call | solution.py:334
  26.6 0.7 %copy.7 = f32[48,16,128]{2,1,0:T(8,128)} copy(f32[48,16,128]{2,1,0:T(8,128)S(1)} %bitcast.6) | data formatting | bytes 786432

commit v8 on v5

--- a/solution.py
+++ b/solution.py
@@ -84,28 +84,25 @@
         place = pl.ds(pl.multiple_of((s * rows + chunk_at(step) * piece) * groups, SUB), block)
         return pltpu.make_async_copy(x_hbm.at[place, :], x_ref.at[place, :], in_sem.at[step, s])
 
-    for step in range(chunks):
-        for s in range(split):
-            fetch(step, s).start()
+    for s in range(split):
+        fetch(0, s).start()
     params = [
         pltpu.make_async_copy(source, target, param_sem.at[i])
         for i, (source, target) in enumerate(
             ((lon_off_hbm, lon_off), (lon_w_hbm, lon_w), (lat_off_hbm, lat_off), (lat_w_hbm, lat_w))
         )
     ]
-    for param in params:
-        param.start()
-
     barrier = pltpu.get_barrier_semaphore()
 
-    def greet(d, carry):
+    distances = [i // 2 + (1 if i % 2 else n // 2) for i in range(n - 1)]
+
+    def peer_at(d):
+        return jnp.where(me + d >= n, me + d - n, me + d)
+
+    for d in distances:
         pl.semaphore_signal(
-            barrier, inc=1, device_id={"lon": lax.rem(me + d, n)},
-            device_id_type=pl.DeviceIdType.MESH,
+            barrier, inc=1, device_id={"lon": peer_at(d)}, device_id_type=pl.DeviceIdType.MESH
         )
-        return carry
-
-    lax.fori_loop(1, n, greet, 0)
 
     def beside(step):
         other = lax.rem(part + step + parts_all, parts_all)
@@ -122,6 +119,12 @@
         pl.semaphore_signal(
             barrier, inc=1, device_id=beside(1), device_id_type=pl.DeviceIdType.MESH
         )
+
+    for step in range(1, chunks):
+        for s in range(split):
+            fetch(step, s).start()
+    for param in params:
+        param.start()
 
     def pack(step):
         for s in range(split):
@@ -144,21 +147,17 @@
         return pl.ds(pl.multiple_of(peer * slot + chunk_at(step) * piece, SUB), piece)
 
     def start_all(source, target, s_sem, r_sem, step):
-        def one(i, carry):
-            peer = lax.rem(me + i // 2 + jnp.where(i % 2 == 0, n // 2, 1), n)
+        place = place_of(me, step)
+        pltpu.make_async_copy(source.at[place, :], target.at[place, :], r_sem.at[step]).start()
+        for d in distances:
             pltpu.make_async_remote_copy(
-                src_ref=source.at[place_of(peer, step), :],
-                dst_ref=target.at[place_of(me, step), :],
+                src_ref=source.at[place_of(peer_at(d), step), :],
+                dst_ref=target.at[place, :],
                 send_sem=s_sem,
                 recv_sem=r_sem.at[step],
-                device_id={"lon": peer},
+                device_id={"lon": peer_at(d)},
                 device_id_type=pl.DeviceIdType.MESH,
             ).start()
-            return carry
-
-        place = place_of(me, step)
-        pltpu.make_async_copy(source.at[place, :], target.at[place, :], r_sem.at[step]).start()
-        lax.fori_loop(0, n - 1, one, 0)
 
     def wait_bytes(ref, sem, count):
         whole = ref.at[pl.ds(0, count), :]

time: 27 us -> 26.9 us (level)
  no operation moved by 1% of the time
where the time goes in v8:
time: 26.9 us; the launch traced here: 26.7 us
  Pallas kernels  26 us (97%)
  local copies, waits for them, and re-layouts  0.75 us (3%)
    pallas_call x1, Pallas kernels, per_device(): pl.pallas_call(functools.partial(kernel, n, bands, groups, share, piece,...  26 us
    unnamed x1, local copies, waits for them, and re-layouts  0.75 us

profile of v8, /device:TPU:0, one launch (start us, length us, event | category | flops | bytes accessed | tf_op | source)
XLA Modules:
  0.0 26.7 jit_solution(9775650728641010977)
XLA Ops:
  0.0 26.0 %shard_map.55 = f32[768,128]{1,0:T(8,128)S(1)} custom-call(f32[768,128]{1,0:T(8,128)} %bitcast.7, s32[4,48]{1,0:T(4,128)} %bitcast.10, f32[4,4,48]{2,1,0:T(4,128)} %bitcast.8, s32[4,48]{1,0:T(4,128)} %bitcast.11, f32[4,4,48]{2,1,0:T(4,128)} %bitcast.9), custom_call_target="tpu_custom_call" | custom-call | tf_op jit(solution)/shard_map/pallas_call | solution.py:326
  26.0 0.7 %copy.7 = f32[48,16,128]{2,1,0:T(8,128)} copy(f32[48,16,128]{2,1,0:T(8,128)S(1)} %bitcast.6) | data formatting | bytes 786432

commit v9 on v8

--- a/solution.py
+++ b/solution.py
@@ -94,7 +94,7 @@
     ]
     barrier = pltpu.get_barrier_semaphore()
 
-    distances = [i // 2 + (1 if i % 2 else n // 2) for i in range(n - 1)]
+    distances = sorted(range(1, n), key=lambda d: -min(d, n - d))
 
     def peer_at(d):
         return jnp.where(me + d >= n, me + d - n, me + d)

time: 26.9 us -> 26.7 us (level)
  no operation moved by 1% of the time
where the time goes in v9:
time: 26.7 us; the launch traced here: 26.6 us
  Pallas kernels  25.8 us (97%)
  local copies, waits for them, and re-layouts  0.75 us (3%)
    pallas_call x1, Pallas kernels, per_device(): pl.pallas_call(functools.partial(kernel, n, bands, groups, share, piece,...  25.8 us
    unnamed x1, local copies, waits for them, and re-layouts  0.75 us

profile of v9, /device:TPU:0, one launch (start us, length us, event | category | flops | bytes accessed | tf_op | source)
XLA Modules:
  0.0 26.6 jit_solution(12407051904536737707)
XLA Ops:
  0.0 25.8 %shard_map.55 = f32[768,128]{1,0:T(8,128)S(1)} custom-call(f32[768,128]{1,0:T(8,128)} %bitcast.7, s32[4,48]{1,0:T(4,128)} %bitcast.10, f32[4,4,48]{2,1,0:T(4,128)} %bitcast.8, s32[4,48]{1,0:T(4,128)} %bitcast.11, f32[4,4,48]{2,1,0:T(4,128)} %bitcast.9), custom_call_target="tpu_custom_call" | custom-call | tf_op jit(solution)/shard_map/pallas_call | solution.py:326
  25.8 0.7 %copy.7 = f32[48,16,128]{2,1,0:T(8,128)} copy(f32[48,16,128]{2,1,0:T(8,128)S(1)} %bitcast.6) | data formatting | bytes 786432
